TPU v7x, 32 devices: a whole 2x2x4 slice. The times are simulated.
32 devices in a mesh: orb: 8 (over y, x, core), probe: 4 (over z).
Axes of the slice: x: 2, y: 2, z: 4, core: 2. Of those that a mesh axis runs over, the one named last changes fastest.
Arguments:
- tiles: bfloat16 [32, 9, 256, 256], P('orb', None, 'probe'), may hold values from -0.0625 to 0.0625
- pattern: int32 [32, 9], P('orb'), may hold values from 0 to 1, as said below
- signs: int32 [8192, 512], P('orb', 'probe'), may hold values from 0 to 1
- previous: bfloat16 [8192, 512], P('orb', 'probe'), may hold values from -6 to 6
- current: bfloat16 [8192, 512], P('orb', 'probe'), may hold values from -6 to 6
Outputs:
- older: bfloat16 [8192, 512], P('orb', 'probe')
- newest: bfloat16 [8192, 512], P('orb', 'probe')
- moments: float32 [4, 512], P(None, 'probe')
Inputs may be any that keep to these rules, and one draw needn't show every extreme that they name: pattern[I, 4] is 1 for every row block; each row block has 4 to 9 ones; the 4 row blocks of one index of orb hold at most 28 ones together, and some index of orb holds exactly 28.
All inputs are finite; a program needn't handle non-finite values.
Results may differ from a plain program's by a relative error of at most 0.0053.
Values may be sent and summed in bfloat16 or wider, within the bound.
A program may use at most 64 MiB of HBM per device.

v0:
```python
import math

import jax
import jax.numpy as jnp
from jax import lax
from jax.sharding import PartitionSpec as P

REACH = 4
STEPS = 4


def extended(array, sides, width):
    for axis, dim in sides:
        peers, length = (lax.axis_size(axis), array.shape[dim])
        up = [(i, (i + 1) % peers) for i in range(peers)]
        down = [(j, i) for i, j in up]
        last = lax.slice_in_dim(array, length - width, length, axis=dim)
        initial = lax.slice_in_dim(array, 0, width, axis=dim)
        before = lax.ppermute(last, axis, up)
        after = lax.ppermute(initial, axis, down)
        array = jnp.concatenate([before, array, after], axis=dim)
    return array


def extend_panel(vec, block_rows):
    return extended(vec, (("orb", 0),), REACH * block_rows)


def body(tiles, pattern, signs, previous, current):
    row_blocks, offsets, shard_rows, block_rows = tiles.shape
    probe_count = previous.shape[1]
    sign_f = (2 * signs - 1).astype(jnp.float32)
    factor = 1.0 / math.sqrt(lax.axis_size("orb") * row_blocks * block_rows)
    full_tiles = lax.all_gather(tiles, "probe", axis=2, tiled=True)
    mask_b = pattern.astype(jnp.bfloat16)
    older, newest = (previous, current)
    collected = []
    for step in range(STEPS):
        blocks = extend_panel(newest, block_rows).reshape(
            row_blocks + 2 * REACH, block_rows, probe_count
        )
        windows = jnp.stack(
            [blocks[offset : offset + row_blocks] for offset in range(offsets)], axis=1
        )
        windows = windows * mask_b[:, :, None, None]
        total = jnp.einsum(
            "roij,rojp->rip", full_tiles, windows, preferred_element_type=jnp.float32
        )
        image = total.reshape(row_blocks * block_rows, probe_count)
        nxt = (2.0 * image - older.astype(jnp.float32)).astype(jnp.bfloat16)
        local_sum = jnp.sum(sign_f * nxt.astype(jnp.float32), axis=0)
        collected.append(lax.psum(local_sum, "orb") * factor)
        older, newest = (newest, nxt)
    stacked = jnp.stack(collected)
    return (older, newest, stacked)


def solution(mesh):
    placed = (
        P("orb", None, "probe", None),
        P("orb", None),
        P("orb", "probe"),
        P("orb", "probe"),
        P("orb", "probe"),
    )
    return jax.shard_map(
        body,
        mesh=mesh,
        in_specs=placed,
        out_specs=(P("orb", "probe"), P("orb", "probe"), P(None, "probe")),
        check_vma=False,
    )
```

profile of v0, /device:TPU:0, one launch (start us, length us, event | category | flops | bytes accessed | tf_op | source)
XLA Modules:
  0.0 224.4 jit_solution(14347151901448904519)
XLA Ops:
  8.4 2.9 %collective-permute-start.1 = (bf16[1024,128]{1,0:T(8,128)(2,1)}, bf16[1024,128]{1,0:T(8,128)(2,1)S(1)}, u32[]{:S(2)}, u32[]{:S(2)}) collective-permute-start(bf16[1024,128]{1,0:T(8,128)(2,1)} %param.9), channel_id=1, source_target_pairs={{4,0},{8,4},{12,8},{16,12},{20,16},{24,20},{28,24},{0,28},{5,1},{9... | collective-permute-start | bytes 786440 | tf_op jit(solution)/shard_map/ppermute | solution.py:20
  11.4 1.1 copy.48
  13.2 2.5 %collective-permute-done = bf16[1024,128]{1,0:T(8,128)(2,1)S(1)} collective-permute-done((bf16[1024,128]{1,0:T(8,128)(2,1)}, bf16[1024,128]{1,0:T(8,128)(2,1)S(1)}, u32[]{:S(2)}, u32[]{:S(2)}) %collective-permute-start) | collective-permute-done | bytes 262176 | tf_op jit(solution)/shard_map/ppermute | solution.py:19
  15.8 1.5 collective-permute-done.1
  23.0 1.1 constant_dynamic-update-slice_fusion.12
  24.1 1.0 constant_dynamic-update-slice_fusion.10
  25.3 76.4 %all-gather.2.cloned.1.call-done = bf16[4,9,256,256]{3,2,1,0:T(8,128)(2,1)} async-done(((bf16[4,9,64,256]{3,2,1,0:T(8,128)(2,1)}), bf16[4,9,256,256]{3,2,1,0:T(8,128)(2,1)}) %all-gather.2.cloned.1.call-update) | async-done | bytes 4718608 | tf_op jit(solution)/shard_map/all_gather | solution.py:34
  101.7 4.0 %fusion.41 = f32[4,256,128]{1,2,0:T(8,128)S(1)} fusion(bf16[4,9,256,256]{3,2,1,0:T(8,128)(2,1)} %all-gather.2.cloned.1.call-done, bf16[4,9,256,128]{2,3,1,0:T(8,128)(2,1)S(1)} %constant_dynamic-update-slice_fusion.4, bf16[4,9]{1,0:T(4,128)(2,1)S(1)} %convert_element_type.38), kind=kOutput, calls=%fused_computation.19 | convolution fusion | flops 605290496 | bytes 7602248 | tf_op jit(solution)/shard_map/roij,rojp->rip/dot_general | solution.py:46
  105.9 1.1 fusion.53
  107.0 2.6 %collective-permute-start.3 = (bf16[1024,128]{1,0:T(8,128)(2,1)S(1)}, bf16[1024,128]{1,0:T(8,128)(2,1)S(1)}, u32[]{:S(2)}, u32[]{:S(2)}) collective-permute-start(bf16[1024,128]{1,0:T(8,128)(2,1)S(1)} %fusion.53), channel_id=1, source_target_pairs={{4,0},{8,4},{12,8},{16,12},{20,16},{24,20},{28,24},{0,28},{5,1},{9... | collective-permute-start | bytes 786440 | tf_op jit(solution)/shard_map/ppermute | solution.py:20
  110.5 4.2 %collective-permute-done.2 = bf16[1024,128]{1,0:T(8,128)(2,1)S(1)} collective-permute-done((bf16[1024,128]{1,0:T(8,128)(2,1)S(1)}, bf16[1024,128]{1,0:T(8,128)(2,1)S(1)}, u32[]{:S(2)}, u32[]{:S(2)}) %collective-permute-start.2) | collective-permute-done | bytes 262176 | tf_op jit(solution)/shard_map/ppermute | solution.py:19
  114.7 1.0 pad_maximum_fusion.4
  118.4 1.8 copy.56
  120.2 1.8 copy.57
  122.0 1.8 copy.59
  123.8 1.8 copy.60
  126.6 1.0 constant_dynamic-update-slice_fusion.20
  127.7 1.0 constant_dynamic-update-slice_fusion.19
  129.6 1.0 constant_dynamic-update-slice_fusion.17
  130.6 1.0 constant_dynamic-update-slice_fusion.16
  131.7 4.0 %fusion.35 = f32[4,256,128]{1,2,0:T(8,128)S(1)} fusion(bf16[4,9,256,256]{3,2,1,0:T(8,128)(2,1)} %all-gather.2.cloned.1.call-done, bf16[4,9,256,128]{2,3,1,0:T(8,128)(2,1)S(1)} %constant_dynamic-update-slice_fusion.13, bf16[4,9]{1,0:T(4,128)(2,1)S(1)} %convert_element_type.38), kind=kOutput, calls=%fused_computation.17 | convolution fusion | flops 605290496 | bytes 7602248 | tf_op jit(solution)/shard_map/roij,rojp->rip/dot_general | solution.py:46
  135.9 1.7 collective-permute-start.4
  137.7 1.1 collective-permute-start.5
  139.6 4.7 %collective-permute-done.4 = bf16[1024,128]{1,0:T(8,128)(2,1)S(1)} collective-permute-done((bf16[1024,128]{1,0:T(8,128)(2,1)S(1)}, bf16[1024,128]{1,0:T(8,128)(2,1)S(1)}, u32[]{:S(2)}, u32[]{:S(2)}) %collective-permute-start.4) | collective-permute-done | bytes 262176 | tf_op jit(solution)/shard_map/ppermute | solution.py:19
  144.4 1.0 pad_maximum_fusion.2
  148.1 1.8 copy.66
  149.9 1.8 copy.67
  151.7 1.8 copy.69
  153.5 1.8 copy.70
  156.3 1.0 constant_dynamic-update-slice_fusion.29
  157.3 1.0 constant_dynamic-update-slice_fusion.28
  159.3 1.0 constant_dynamic-update-slice_fusion.26
  161.3 4.8 %fusion.29 = f32[4,256,128]{1,2,0:T(8,128)} fusion(bf16[4,9,256,256]{3,2,1,0:T(8,128)(2,1)} %all-gather.2.cloned.1.call-done, bf16[4,9,256,128]{2,3,1,0:T(8,128)(2,1)S(1)} %constant_dynamic-update-slice_fusion.22, bf16[4,9]{1,0:T(4,128)(2,1)S(1)} %convert_element_type.38), kind=kOutput, calls=%fused_computation.15 | convolution fusion | flops 605290496 | bytes 7602248 | tf_op jit(solution)/shard_map/roij,rojp->rip/dot_general | solution.py:46
  166.1 1.2 copy.73
  167.5 2.0 collective-permute-start.6
  171.0 5.2 %collective-permute-done.6 = bf16[1024,128]{1,0:T(8,128)(2,1)S(1)} collective-permute-done((bf16[1024,128]{1,0:T(8,128)(2,1)S(1)}, bf16[1024,128]{1,0:T(8,128)(2,1)S(1)}, u32[]{:S(2)}, u32[]{:S(2)}) %collective-permute-start.6) | collective-permute-done | bytes 262176 | tf_op jit(solution)/shard_map/ppermute | solution.py:19
  176.2 1.2 pad_maximum_fusion
  180.0 1.8 copy.76
  181.8 1.8 copy.77
  183.6 1.8 copy.79
  185.4 1.8 copy.80
  187.2 1.8 copy.81
  189.9 1.0 constant_dynamic-update-slice_fusion.38
  190.9 1.0 constant_dynamic-update-slice_fusion.37
  194.9 4.8 %fusion.23 = f32[4,256,128]{1,2,0:T(8,128)} fusion(bf16[4,9,256,256]{3,2,1,0:T(8,128)(2,1)} %all-gather.2.cloned.1.call-done, bf16[4,9,256,128]{2,3,1,0:T(8,128)(2,1)S(1)} %constant_dynamic-update-slice_fusion.31, bf16[4,9]{1,0:T(4,128)(2,1)S(1)} %convert_element_type.38), kind=kOutput, calls=%fused_computation.13 | convolution fusion | flops 605290496 | bytes 7602248 | tf_op jit(solution)/shard_map/roij,rojp->rip/dot_general | solution.py:46
  199.7 1.2 copy.83
  201.0 2.0 fusion.49
  203.0 13.9 %all-reduce = (f32[128]{0:T(128)S(1)}, f32[128]{0:T(128)S(1)}, f32[128]{0:T(128)S(1)}, f32[128]{0:T(128)S(1)}) all-reduce(f32[128]{0:T(128)S(1)} %get-tuple-element.4, f32[128]{0:T(128)S(1)} %get-tuple-element.5, f32[128]{0:T(128)S(1)} %get-tuple-element.6, f32[128]{0:T(128)S(1)} %get-tuple-element.3), channel_id=1, replica_groups=mesh['orb'=8,'probe'=4] {'orb'}, use_global_device_ids=true, to_apply=%region_7.0 | all-reduce | flops 512 | bytes 4096 | tf_op jit(solution)/shard_map/psum | solution.py:52
  (95 shorter events, 29.1 us)
Async XLA Ops:
  7.2 8.6 %copy-start.1 = (bf16[1024,128]{1,0:T(8,128)(2,1)S(1)}, bf16[1024,128]{1,0:T(8,128)(2,1)}, u32[]{:S(2)}) copy-start(bf16[1024,128]{1,0:T(8,128)(2,1)} %param.9) | copy-start | bytes 786436
  7.2 94.5 %all-gather.2.cloned.1.call-start = ((), (), s32[]{:S(2)}) async-start(), calls=%async_computation | async-start | bytes 5898240 | tf_op jit(solution)/shard_map/all_gather | solution.py:34
  7.9 7.8 %collective-permute-start = (bf16[1024,128]{1,0:T(8,128)(2,1)}, bf16[1024,128]{1,0:T(8,128)(2,1)S(1)}, u32[]{:S(2)}, u32[]{:S(2)}) collective-permute-start(bf16[1024,128]{1,0:T(8,128)(2,1)} %param.9), channel_id=1, source_target_pairs={{0,4},{4,8},{8,12},{12,16},{16,20},{20,24},{24,28},{28,0},{1,5},{5... | collective-permute-start | bytes 786440 | tf_op jit(solution)/shard_map/ppermute | solution.py:19
  8.4 8.9 %collective-permute-start.1 = (bf16[1024,128]{1,0:T(8,128)(2,1)}, bf16[1024,128]{1,0:T(8,128)(2,1)S(1)}, u32[]{:S(2)}, u32[]{:S(2)}) collective-permute-start(bf16[1024,128]{1,0:T(8,128)(2,1)} %param.9), channel_id=1, source_target_pairs={{4,0},{8,4},{12,8},{16,12},{20,16},{24,20},{28,24},{0,28},{5,1},{9... | collective-permute-start | bytes 786440 | tf_op jit(solution)/shard_map/ppermute | solution.py:20
  23.0 2.1 copy-start.5
  23.0 2.2 copy-start.3
  23.0 2.2 copy-start.4
  23.0 2.2 copy-start.2
  107.0 7.7 %collective-permute-start.2 = (bf16[1024,128]{1,0:T(8,128)(2,1)S(1)}, bf16[1024,128]{1,0:T(8,128)(2,1)S(1)}, u32[]{:S(2)}, u32[]{:S(2)}) collective-permute-start(bf16[1024,128]{1,0:T(8,128)(2,1)S(1)} %fusion.53), channel_id=1, source_target_pairs={{0,4},{4,8},{8,12},{12,16},{16,20},{20,24},{24,28},{28,0},{1,5},{5... | collective-permute-start | bytes 786440 | tf_op jit(solution)/shard_map/ppermute | solution.py:19
  107.0 7.7 %collective-permute-start.3 = (bf16[1024,128]{1,0:T(8,128)(2,1)S(1)}, bf16[1024,128]{1,0:T(8,128)(2,1)S(1)}, u32[]{:S(2)}, u32[]{:S(2)}) collective-permute-start(bf16[1024,128]{1,0:T(8,128)(2,1)S(1)} %fusion.53), channel_id=1, source_target_pairs={{4,0},{8,4},{12,8},{16,12},{20,16},{24,20},{28,24},{0,28},{5,1},{9... | collective-permute-start | bytes 786440 | tf_op jit(solution)/shard_map/ppermute | solution.py:20
  126.6 4.9 %copy-start.7 = (bf16[4,1,256,128]{2,3,1,0:T(8,128)(2,1)S(1)}, bf16[4,1,256,128]{2,3,1,0:T(8,128)(2,1)}, u32[]{:S(2)}) copy-start(bf16[4,1,256,128]{2,3,1,0:T(8,128)(2,1)} %copy.60) | copy-start | bytes 786436
  126.6 5.0 %copy-start.8 = (bf16[4,1,256,128]{2,3,1,0:T(8,128)(2,1)S(1)}, bf16[4,1,256,128]{2,3,1,0:T(8,128)(2,1)}, u32[]{:S(2)}) copy-start(bf16[4,1,256,128]{2,3,1,0:T(8,128)(2,1)} %copy.61) | copy-start | bytes 786436
  135.9 8.4 %collective-permute-start.4 = (bf16[1024,128]{1,0:T(8,128)(2,1)S(1)}, bf16[1024,128]{1,0:T(8,128)(2,1)S(1)}, u32[]{:S(2)}, u32[]{:S(2)}) collective-permute-start(bf16[1024,128]{1,0:T(8,128)(2,1)S(1)} %fusion.52), channel_id=1, source_target_pairs={{0,4},{4,8},{8,12},{12,16},{16,20},{20,24},{24,28},{28,0},{1,5},{5... | collective-permute-start | bytes 786440 | tf_op jit(solution)/shard_map/ppermute | solution.py:19
  137.7 6.7 %collective-permute-start.5 = (bf16[1024,128]{1,0:T(8,128)(2,1)S(1)}, bf16[1024,128]{1,0:T(8,128)(2,1)S(1)}, u32[]{:S(2)}, u32[]{:S(2)}) collective-permute-start(bf16[1024,128]{1,0:T(8,128)(2,1)S(1)} %fusion.52), channel_id=1, source_target_pairs={{4,0},{8,4},{12,8},{16,12},{20,16},{24,20},{28,24},{0,28},{5,1},{9... | collective-permute-start | bytes 786440 | tf_op jit(solution)/shard_map/ppermute | solution.py:20
  156.3 4.9 %copy-start.9 = (bf16[4,1,256,128]{2,3,1,0:T(8,128)(2,1)S(1)}, bf16[4,1,256,128]{2,3,1,0:T(8,128)(2,1)}, u32[]{:S(2)}) copy-start(bf16[4,1,256,128]{2,3,1,0:T(8,128)(2,1)} %copy.70) | copy-start | bytes 786436
  156.3 5.0 %copy-start.10 = (bf16[4,1,256,128]{2,3,1,0:T(8,128)(2,1)S(1)}, bf16[4,1,256,128]{2,3,1,0:T(8,128)(2,1)}, u32[]{:S(2)}) copy-start(bf16[4,1,256,128]{2,3,1,0:T(8,128)(2,1)} %copy.71) | copy-start | bytes 786436
  167.4 33.5 %copy-start = (bf16[1024,128]{1,0:T(8,128)(2,1)}, bf16[1024,128]{1,0:T(8,128)(2,1)S(1)}, u32[]{:S(2)}) copy-start(bf16[1024,128]{1,0:T(8,128)(2,1)S(1)} %fusion.48) | copy-start | bytes 786436
  167.5 8.7 %collective-permute-start.6 = (bf16[1024,128]{1,0:T(8,128)(2,1)S(1)}, bf16[1024,128]{1,0:T(8,128)(2,1)S(1)}, u32[]{:S(2)}, u32[]{:S(2)}) collective-permute-start(bf16[1024,128]{1,0:T(8,128)(2,1)S(1)} %fusion.48), channel_id=1, source_target_pairs={{0,4},{4,8},{8,12},{12,16},{16,20},{20,24},{24,28},{28,0},{1,5},{5... | collective-permute-start | bytes 786440 | tf_op jit(solution)/shard_map/ppermute | solution.py:19
  169.5 6.7 %collective-permute-start.7 = (bf16[1024,128]{1,0:T(8,128)(2,1)S(1)}, bf16[1024,128]{1,0:T(8,128)(2,1)S(1)}, u32[]{:S(2)}, u32[]{:S(2)}) collective-permute-start(bf16[1024,128]{1,0:T(8,128)(2,1)S(1)} %fusion.48), channel_id=1, source_target_pairs={{4,0},{8,4},{12,8},{16,12},{20,16},{24,20},{28,24},{0,28},{5,1},{9... | collective-permute-start | bytes 786440 | tf_op jit(solution)/shard_map/ppermute | solution.py:20
  189.9 4.9 %copy-start.11 = (bf16[4,1,256,128]{2,3,1,0:T(8,128)(2,1)S(1)}, bf16[4,1,256,128]{2,3,1,0:T(8,128)(2,1)}, u32[]{:S(2)}) copy-start(bf16[4,1,256,128]{2,3,1,0:T(8,128)(2,1)} %copy.80) | copy-start | bytes 786436
  189.9 5.0 %copy-start.12 = (bf16[4,1,256,128]{2,3,1,0:T(8,128)(2,1)S(1)}, bf16[4,1,256,128]{2,3,1,0:T(8,128)(2,1)}, u32[]{:S(2)}) copy-start(bf16[4,1,256,128]{2,3,1,0:T(8,128)(2,1)} %copy.81) | copy-start | bytes 786436
  189.9 5.0 %copy-start.6 = (bf16[4,1,256,128]{2,3,1,0:T(8,128)(2,1)S(1)}, bf16[4,1,256,128]{2,3,1,0:T(8,128)(2,1)}, u32[]{:S(2)}) copy-start(bf16[4,1,256,128]{2,3,1,0:T(8,128)(2,1)} %copy.82) | copy-start | bytes 786436
Sparse Core Ops, SparseCore 0:
  9.6 92.0 all-gather.1
where the time goes:
time: 226 us; the launch traced here: 224 us
  waiting for transfers between devices  95.2 us (42%)
  local copies, waits for them, and re-layouts  63.6 us (28%)
  matrix products  17.6 us (8%)
  between operations  14.6 us (6%)
  blocking collectives  13.9 us (6%)
  starting transfers between devices  11.7 us (5%)
  other arithmetic  7.73 us (3%)
    all_gather x1, waiting for transfers between devices, body(): full_tiles = lax.all_gather(tiles, 'probe', axis=2, tiled=True)  76.4 us
    another operation x40, local copies, waits for them, and re-layouts, body(): jnp.stack([blocks[offset:offset + row_blocks] for offset in range(offsets...  40.6 us
    unnamed x60, local copies, waits for them, and re-layouts  20 us
    dot_general x4, matrix products, body(): jnp.einsum('roij,rojp->rip', full_tiles, windows, preferred_element_type=...  17.6 us
    ppermute x4, waiting for transfers between devices, extended(): before = lax.ppermute(last, axis, up)  16.6 us
    psum x1, blocking collectives, body(): collected.append(lax.psum(local_sum, 'orb') * factor)  13.9 us
    ppermute x4, starting transfers between devices, extended(): after = lax.ppermute(initial, axis, down)  7.37 us
  transfers between devices with their start and end apart: 9, of which 6 were waited for; matrix products, arithmetic and copies ran while one was open for 5% of the time, Pallas kernels for 0%

commit v1 on v0

v1 whole, which is shorter than its diff:
```python
import functools
import math

import jax
import jax.numpy as jnp
from jax import lax
from jax.experimental import pallas as pl
from jax.experimental.pallas import tpu as pltpu
from jax.sharding import PartitionSpec as P

STEPS = 4
LIVE_PER_ROW = 7
LEAST_PER_ROW = 4
MESH = pl.DeviceIdType.MESH


def chunk_bounds(row_blocks, offsets):
    slots = LIVE_PER_ROW * row_blocks
    return [
        min(offsets * (i + 1), slots - LEAST_PER_ROW * (row_blocks - 1 - i))
        for i in range(row_blocks)
    ]


def kernel(
    n_orb, n_probe, rb, offs, rows, bs, pc,
    pattern_ref, tiles_hbm, signs_hbm, previous_hbm, current_hbm,
    older_hbm, newest_hbm, moments_ref,
    tl, signs, prev, full, stage, dense, win, last, acc, mbuf, slot_of, nxt,
    in_sem, out_sem, g_send, g_recv, h_send, h_recv, m_send, m_recv,
):
    slots = LIVE_PER_ROW * rb
    span = rb * bs
    depth = offs * bs
    bounds = chunk_bounds(rb, offs)
    chunks = list(zip([0] + bounds[:-1], bounds))
    orb = lax.axis_index("orb")
    z = lax.axis_index("probe")
    up = lax.rem(orb + 1, n_orb)
    down = lax.rem(orb + n_orb - 1, n_orb)

    loads = [
        pltpu.make_async_copy(tiles_hbm, tl, in_sem.at[0]),
        pltpu.make_async_copy(current_hbm, win.at[0, pl.ds(span, span)], in_sem.at[1]),
        pltpu.make_async_copy(previous_hbm, prev, in_sem.at[2]),
        pltpu.make_async_copy(signs_hbm, signs, in_sem.at[3]),
    ]
    for load in loads:
        load.start()

    barrier = pltpu.get_barrier_semaphore()

    def greet(j, carry):
        pl.semaphore_signal(
            barrier, inc=1, device_id=(lax.rem(orb + j, n_orb), z), device_id_type=MESH
        )
        return carry

    lax.fori_loop(1, n_orb, greet, 0)

    @pl.when(z > 0)
    def _():
        pl.semaphore_signal(barrier, inc=1, device_id=(orb, z - 1), device_id_type=MESH)

    @pl.when(z < n_probe - 1)
    def _():
        pl.semaphore_signal(barrier, inc=1, device_id=(orb, z + 1), device_id_type=MESH)

    count = jnp.int32(0)
    for j in range(rb * offs):
        live = pattern_ref[j // offs, j % offs] == 1
        slot_of[j] = jnp.where(live, count, slots)
        count = count + live.astype(jnp.int32)
    following = jnp.int32(rb * offs - 1)
    nxt[rb * offs] = following
    for j in reversed(range(rb * offs)):
        live = pattern_ref[j // offs, j % offs] == 1
        following = jnp.where(live, j, following)
        nxt[j] = following
    stage[slots] = jnp.zeros((rows, bs), stage.dtype)

    loads[0].wait()
    at = nxt[0]
    for s in range(slots):
        full[z, s] = tl[at]
        at = nxt[at + 1]

    ends = (z > 0).astype(jnp.int32) + (z < n_probe - 1).astype(jnp.int32)
    pl.semaphore_wait(barrier, n_orb - 1 + ends)

    def tile_copy(side, d, c, q):
        lo, hi = chunks[c]
        piece = full.at[q, pl.ds(lo, hi - lo)]
        to = z + 1 if side == 0 else z - 1
        return pltpu.make_async_remote_copy(
            src_ref=piece, dst_ref=piece,
            send_sem=g_send.at[side, d - 1], recv_sem=g_recv.at[side, d - 1, c],
            device_id=(orb, to), device_id_type=MESH,
        )

    has_next = (z < n_probe - 1, z > 0)
    for c in range(rb):
        for side in range(2):
            @pl.when(has_next[side])
            def _():
                tile_copy(side, 1, c, z).start()

    def halo_copy(k, way, start, size):
        src = win.at[k, pl.ds(span + start, size)]
        dst = win.at[k, pl.ds((0 if way == 0 else 2 * span) + start, size)]
        return pltpu.make_async_remote_copy(
            src_ref=src, dst_ref=dst,
            send_sem=h_send.at[k, way], recv_sem=h_recv.at[k, way],
            device_id=(up if way == 0 else down, z), device_id_type=MESH,
        )

    loads[1].wait()
    for way in range(2):
        halo_copy(0, way, 0, span).start()
    loads[2].wait()

    def first_step(i, q):
        base = pl.multiple_of(q * rows, rows)
        total = jnp.dot(
            dense[i, pl.ds(base, rows), :],
            win[0, pl.ds(i * bs, depth), :],
            preferred_element_type=jnp.float32,
        )
        here = pl.multiple_of(i * bs + q * rows, rows)
        before = prev[pl.ds(here, rows), :].astype(jnp.float32)
        win[1, pl.ds(pl.multiple_of(span + here, rows), rows), :] = (
            2.0 * total - before
        ).astype(win.dtype)
        for way in range(2):
            halo_copy(1, way, here, rows).start()

    base_z = pl.multiple_of(z * rows, rows)
    for i in range(rb):
        for o in range(offs):
            mask = pattern_ref[i, o].astype(jnp.float32).astype(tl.dtype)
            dense[i, pl.ds(base_z, rows), o * bs:(o + 1) * bs] = tl[i * offs + o] * mask
    for way in range(2):
        halo_copy(0, way, 0, span).wait_recv()
    for i in range(rb):
        first_step(i, z)

    def hop(d, carry):
        for c in range(rb):
            lo, hi = chunks[c]
            for side in range(2):
                q = z - d if side == 0 else z + d
                valid = q >= 0 if side == 0 else q < n_probe

                @pl.when(valid)
                def _():
                    tile_copy(side, d, c, q).wait_recv()

                    @pl.when(has_next[side])
                    def _():
                        tile_copy(side, d + 1, c, q).start()

            for side in range(2):
                q = z - d if side == 0 else z + d
                valid = q >= 0 if side == 0 else q < n_probe

                @pl.when(valid)
                def _():
                    for s in range(lo, hi):
                        stage[s + side * (slots + 1)] = full[q, s]
                    base = pl.multiple_of(q * rows, rows)
                    for o in range(offs):
                        dense[c, pl.ds(base, rows), o * bs:(o + 1) * bs] = stage[
                            slot_of[c * offs + o] + side * (slots + 1)
                        ]
                    first_step(c, q)
        return carry

    stage[2 * slots + 1] = jnp.zeros((rows, bs), stage.dtype)
    lax.fori_loop(1, n_probe, hop, 0)
    loads[3].wait()

    def moment(value, start):
        sign = (2 * signs[pl.ds(start, bs), :] - 1).astype(jnp.float32)
        return jnp.sum(sign * value.astype(jnp.float32), axis=0, keepdims=True)

    def dot(i, first, blocks, k):
        return jnp.dot(
            dense[i, :, (first - i) * bs:(first - i + blocks) * bs],
            win[k, pl.ds(first * bs, blocks * bs), :],
            preferred_element_type=jnp.float32,
        )

    sums = []
    outs = []
    for k in range(2, STEPS + 1):
        for i in range(rb):
            acc[i] = dot(i, rb, rb, k - 1)
        total = jnp.zeros((1, pc), jnp.float32)
        for i in range(rb):
            total += moment(win[k - 1, pl.ds(span + i * bs, bs), :], i * bs)
        sums.append(total)
        for way in range(2):
            halo_copy(k - 1, way, 0, span).wait_recv()
        last_sum = jnp.zeros((1, pc), jnp.float32)
        for i in range(rb):
            image = acc[i] + dot(i, i, rb - i, k - 1) + dot(i, 2 * rb, i + 1, k - 1)
            before = win[k - 2, pl.ds(span + i * bs, bs), :].astype(jnp.float32)
            value = (2.0 * image - before).astype(win.dtype)
            if k < STEPS:
                win[k, pl.ds(span + i * bs, bs), :] = value
                for way in range(2):
                    halo_copy(k, way, i * bs, bs).start()
            else:
                last[pl.ds(i * bs, bs), :] = value
                last_sum += moment(value, i * bs)
        if k == STEPS - 1:
            outs.append(
                pltpu.make_async_copy(win.at[k, pl.ds(span, span)], older_hbm, out_sem.at[0])
            )
            outs[-1].start()
        if k == STEPS:
            sums.append(last_sum)
            outs.append(pltpu.make_async_copy(last, newest_hbm, out_sem.at[1]))
            outs[-1].start()

    mbuf[orb, 0:STEPS, :] = jnp.concatenate(sums, axis=0)

    def moment_copy(j):
        return pltpu.make_async_remote_copy(
            src_ref=mbuf.at[orb], dst_ref=mbuf.at[orb],
            send_sem=m_send, recv_sem=m_recv,
            device_id=(lax.rem(orb + j, n_orb), z), device_id_type=MESH,
        )

    def send_moment(j, carry):
        moment_copy(j).start()
        return carry

    lax.fori_loop(1, n_orb, send_moment, 0)

    for k in range(STEPS):
        for way in range(2):
            halo_copy(k, way, 0, span).wait_send()

    def sent(d, carry):
        for side in range(2):
            q = z + 1 - d if side == 0 else z - 1 + d
            valid = q >= 0 if side == 0 else q < n_probe

            @pl.when(jnp.logical_and(valid, has_next[side]))
            def _():
                pltpu.make_async_remote_copy(
                    src_ref=full.at[q], dst_ref=full.at[q],
                    send_sem=g_send.at[side, d - 1], recv_sem=g_recv.at[side, d - 1, 0],
                    device_id=(orb, z + 1 if side == 0 else z - 1), device_id_type=MESH,
                ).wait_send()
        return carry

    lax.fori_loop(1, n_probe, sent, 0)

    others = mbuf.at[pl.ds(0, n_orb - 1)]
    arrived = pltpu.make_async_remote_copy(
        src_ref=others, dst_ref=others, send_sem=m_send, recv_sem=m_recv,
        device_id=(up, z), device_id_type=MESH,
    )
    arrived.wait_recv()
    arrived.wait_send()
    result = mbuf[0]
    for j in range(1, n_orb):
        result = result + mbuf[j]
    moments_ref[...] = result[0:STEPS] * (1.0 / math.sqrt(n_orb * span))
    for out in outs:
        out.wait()


def body(tiles, pattern, signs, previous, current):
    n_orb, n_probe = lax.axis_size("orb"), lax.axis_size("probe")
    rb, offs, rows, bs = tiles.shape
    pc = previous.shape[1]
    slots = LIVE_PER_ROW * rb
    span = rb * bs
    bf16, f32 = jnp.bfloat16, jnp.float32
    anywhere = pl.BlockSpec(memory_space=pl.ANY)
    older, newest, moments = pl.pallas_call(
        functools.partial(kernel, n_orb, n_probe, rb, offs, rows, bs, pc),
        out_shape=(
            jax.ShapeDtypeStruct((span, pc), bf16),
            jax.ShapeDtypeStruct((span, pc), bf16),
            jax.ShapeDtypeStruct((STEPS, pc), f32),
        ),
        in_specs=[pl.BlockSpec(memory_space=pltpu.SMEM)] + [anywhere] * 4,
        out_specs=(anywhere, anywhere, pl.BlockSpec(memory_space=pltpu.VMEM)),
        scratch_shapes=[
            pltpu.VMEM((rb * offs, rows, bs), bf16),
            pltpu.VMEM((span, pc), jnp.int32),
            pltpu.VMEM((span, pc), bf16),
            pltpu.VMEM((n_probe, slots, rows, bs), bf16),
            pltpu.VMEM((2 * (slots + 1), rows, bs), bf16),
            pltpu.VMEM((rb, bs, offs * bs), bf16),
            pltpu.VMEM((STEPS, 3 * span, pc), bf16),
            pltpu.VMEM((span, pc), bf16),
            pltpu.VMEM((rb, bs, pc), f32),
            pltpu.VMEM((n_orb, 8, pc), f32),
            pltpu.SMEM((rb * offs,), jnp.int32),
            pltpu.SMEM((rb * offs + 1,), jnp.int32),
            pltpu.SemaphoreType.DMA((4,)),
            pltpu.SemaphoreType.DMA((2,)),
            pltpu.SemaphoreType.DMA((2, n_probe - 1)),
            pltpu.SemaphoreType.DMA((2, n_probe - 1, rb)),
            pltpu.SemaphoreType.DMA((STEPS, 2)),
            pltpu.SemaphoreType.DMA((STEPS, 2)),
            pltpu.SemaphoreType.DMA,
            pltpu.SemaphoreType.DMA,
        ],
        compiler_params=pltpu.CompilerParams(
            collective_id=0, has_side_effects=True, vmem_limit_bytes=40 * 2**20
        ),
    )(pattern, tiles.reshape(rb * offs, rows, bs), signs, previous, current)
    return older, newest, moments


def solution(mesh):
    placed = (
        P("orb", None, "probe", None),
        P("orb", None),
        P("orb", "probe"),
        P("orb", "probe"),
        P("orb", "probe"),
    )
    return jax.shard_map(
        body,
        mesh=mesh,
        in_specs=placed,
        out_specs=(P("orb", "probe"), P("orb", "probe"), P(None, "probe")),
        check_vma=False,
    )
```

time: 226 us -> 96.9 us (0.43)
  waiting for transfers between devices: 95.2 us -> 0 us
  Pallas kernels: 0 us -> 89.1 us
  local copies, waits for them, and re-layouts: 63.6 us -> 6.87 us
  matrix products: 17.6 us -> 0 us
  between operations: 14.6 us -> 0.65 us
  blocking collectives: 13.9 us -> 0 us
  starting transfers between devices: 11.7 us -> 0 us
  other arithmetic: 7.73 us -> 0 us
    pallas_call x0 -> x1, Pallas kernels: none -> 89.1 us  [body(): pl.pallas_call(functools.partial(kernel, n_orb, n_probe, rb, offs, rows,...]
    all_gather x1 -> x0, waiting for transfers between devices: 76.4 us -> none  [body(): full_tiles = lax.all_gather(tiles, 'probe', axis=2, tiled=True)]
    another operation x40 -> x0, local copies, waits for them, and re-layouts: 40.6 us -> none  [body(): jnp.stack([blocks[offset:offset + row_blocks] for offset in range(offsets...]
    ppermute x8 -> x0, waiting for transfers between devices: 18.1 us -> none  [the longest x4 16.6 us: extended(): before = lax.ppermute(last, axis, up)]
    dot_general x4 -> x0, matrix products: 17.6 us -> none  [body(): jnp.einsum('roij,rojp->rip', full_tiles, windows, preferred_element_type=...]
    psum x1 -> x0, blocking collectives: 13.9 us -> none  [body(): collected.append(lax.psum(local_sum, 'orb') * factor)]
    unnamed x60 -> x13, local copies, waits for them, and re-layouts: 20 us -> 6.87 us
    ppermute x8 -> x0, starting transfers between devices: 11.7 us -> none  [the longest x4 7.37 us: extended(): after = lax.ppermute(initial, axis, down)]
  transfers between devices with their start and end apart: 9 -> 0, of which waited for: 6 -> 0; matrix products, arithmetic and copies ran while one was open for 5% -> 0% of each run, Pallas kernels for 0% -> 0%
where the time goes in v1:
time: 96.9 us; the launch traced here: 96.6 us
  Pallas kernels  89.1 us (92%)
  local copies, waits for them, and re-layouts  6.87 us (7%)
    pallas_call x1, Pallas kernels, body(): pl.pallas_call(functools.partial(kernel, n_orb, n_probe, rb, offs, rows,...  89.1 us
    unnamed x13, local copies, waits for them, and re-layouts  6.87 us

profile of v1, /device:TPU:0, one launch (start us, length us, event | category | flops | bytes accessed | tf_op | source)
XLA Modules:
  0.0 96.6 jit_solution(13965480100416139361)
XLA Ops:
  0.6 0.0 copy-start
  0.6 1.3 %copy-done = bf16[4,9,64,256]{3,2,1,0:T(8,128)(2,1)S(1)} copy-done((bf16[4,9,64,256]{3,2,1,0:T(8,128)(2,1)S(1)}, bf16[4,9,64,256]{3,2,1,0:T(8,128)(2,1)}, u32[]{:S(2)}) %copy-start) | copy-done | bytes 1179672
  1.9 0.0 copy-start.1
  1.9 1.0 %copy-done.1 = s32[1024,128]{1,0:T(8,128)S(1)} copy-done((s32[1024,128]{1,0:T(8,128)S(1)}, s32[1024,128]{1,0:T(8,128)}, u32[]{:S(2)}) %copy-start.1) | copy-done | bytes 524312
  2.9 0.0 copy-start.2
  2.9 0.9 copy-done.2
  3.9 0.0 copy-start.3
  3.9 0.9 copy-done.3
  4.8 0.0 copy-start.4
  4.8 0.7 copy-done.4
  5.5 89.1 %shard_map.76 = (bf16[1024,128]{1,0:T(8,128)(2,1)S(1)}, bf16[1024,128]{1,0:T(8,128)(2,1)S(1)}, f32[4,128]{1,0:T(4,128)S(1)}) custom-call(s32[4,9]{1,0:T(4,128)S(1)} %copy-done.4, bf16[36,64,256]{2,1,0:T(8,128)(2,1)S(1)} %bitcast.1, s32[1024,128]{1,0:T(8,128)S(1)} %copy-done.1, bf16[1024,128]{1,0:T(8,128)(2,1)S(1)} %copy-done.2, bf16[1024,128]{1,0:T(8,128)(2,1)S(1)} %copy-done.3), custom_call_target="tpu_custom_call" | custom-call | tf_op jit(solution)/shard_map/pallas_call | solution.py:284
  94.6 0.7 copy.11
  95.3 0.7 copy.12
  96.0 0.6 copy.13
Async XLA Ops:
  0.6 1.3 %copy-start = (bf16[4,9,64,256]{3,2,1,0:T(8,128)(2,1)S(1)}, bf16[4,9,64,256]{3,2,1,0:T(8,128)(2,1)}, u32[]{:S(2)}) copy-start(bf16[4,9,64,256]{3,2,1,0:T(8,128)(2,1)} %param.5) | copy-start | bytes 3538948
  1.9 1.0 %copy-start.1 = (s32[1024,128]{1,0:T(8,128)S(1)}, s32[1024,128]{1,0:T(8,128)}, u32[]{:S(2)}) copy-start(s32[1024,128]{1,0:T(8,128)} %signs_hbm.1) | copy-start | bytes 1572868
  2.9 0.9 copy-start.2
  3.9 0.9 copy-start.3
  4.8 0.7 copy-start.4

commit v2 on v1

--- a/solution.py
+++ b/solution.py
@@ -24,10 +24,11 @@
 
 def kernel(
     n_orb, n_probe, rb, offs, rows, bs, pc,
-    pattern_ref, tiles_hbm, signs_hbm, previous_hbm, current_hbm,
+    pattern_hbm, tiles_hbm, signs_hbm, previous_hbm, current_hbm,
     older_hbm, newest_hbm, moments_ref,
-    tl, signs, prev, full, stage, dense, win, last, acc, mbuf, slot_of, nxt,
+    tl, signs, prev, full, stage, dense, win, last, acc, mbuf, hwin, hprev, hout, pattern_ref, slot_of, nxt,
     in_sem, out_sem, g_send, g_recv, h_send, h_recv, m_send, m_recv,
+    e_send, e_recv, eh_send, eh_recv, r_send, r_recv,
 ):
     slots = LIVE_PER_ROW * rb
     span = rb * bs
@@ -44,6 +45,7 @@
         pltpu.make_async_copy(current_hbm, win.at[0, pl.ds(span, span)], in_sem.at[1]),
         pltpu.make_async_copy(previous_hbm, prev, in_sem.at[2]),
         pltpu.make_async_copy(signs_hbm, signs, in_sem.at[3]),
+        pltpu.make_async_copy(pattern_hbm, pattern_ref, in_sem.at[4]),
     ]
     for load in loads:
         load.start()
@@ -66,6 +68,7 @@
     def _():
         pl.semaphore_signal(barrier, inc=1, device_id=(orb, z + 1), device_id_type=MESH)
 
+    loads[4].wait()
     count = jnp.int32(0)
     for j in range(rb * offs):
         live = pattern_ref[j // offs, j % offs] == 1
@@ -105,6 +108,50 @@
             def _():
                 tile_copy(side, 1, c, z).start()
 
+    low = z < n_probe // 2
+    is_end = jnp.logical_or(z == 0, z == n_probe - 1)
+    helps = jnp.logical_or(z == 1, z == n_probe - 2)
+    partner = jnp.where(
+        is_end, jnp.where(low, 1, n_probe - 2), jnp.where(low, 0, n_probe - 1)
+    )
+    far = jnp.where(low, n_probe - 1, 0)
+
+    def lend_copy(src, dst, which):
+        return pltpu.make_async_remote_copy(
+            src_ref=src, dst_ref=dst,
+            send_sem=e_send.at[which], recv_sem=e_recv.at[which],
+            device_id=(orb, partner), device_id_type=MESH,
+        )
+
+    def lent_vec():
+        return lend_copy(win.at[0, pl.ds(span, span)], hwin.at[pl.ds(span, span)], 0)
+
+    def lent_prev(start, size):
+        return lend_copy(prev.at[pl.ds(start, size)], hprev.at[pl.ds(start, size)], 1)
+
+    def lent_halo(way):
+        return pltpu.make_async_remote_copy(
+            src_ref=hwin.at[pl.ds(span, span)],
+            dst_ref=hwin.at[pl.ds(0 if way == 0 else 2 * span, span)],
+            send_sem=eh_send.at[way], recv_sem=eh_recv.at[way],
+            device_id=(up if way == 0 else down, z), device_id_type=MESH,
+        )
+
+    def help_copy(c):
+        row = pl.multiple_of(span + c * bs + far * rows, rows)
+        return pltpu.make_async_remote_copy(
+            src_ref=hout.at[c], dst_ref=win.at[1, pl.ds(row, rows)],
+            send_sem=r_send, recv_sem=r_recv,
+            device_id=(orb, partner), device_id_type=MESH,
+        )
+
+    def all_help():
+        whole = prev.at[pl.ds(0, rb * rows)]
+        return pltpu.make_async_remote_copy(
+            src_ref=whole, dst_ref=whole, send_sem=r_send, recv_sem=r_recv,
+            device_id=(orb, partner), device_id_type=MESH,
+        )
+
     def halo_copy(k, way, start, size):
         src = win.at[k, pl.ds(span + start, size)]
         dst = win.at[k, pl.ds((0 if way == 0 else 2 * span) + start, size)]
@@ -119,20 +166,50 @@
         halo_copy(0, way, 0, span).start()
     loads[2].wait()
 
-    def first_step(i, q):
+    @pl.when(is_end)
+    def _():
+        lent_vec().start()
+        for i in range(rb):
+            lent_prev(pl.multiple_of(i * bs + far * rows, rows), rows).start()
+
+    def piece(k, i, start, size):
+        total = jnp.dot(
+            dense[i, pl.ds(start, size), :],
+            win[k - 1, pl.ds(i * bs, depth), :],
+            preferred_element_type=jnp.float32,
+        )
+        here = pl.multiple_of(i * bs + start, rows)
+        there = pl.multiple_of(span + here, rows)
+        if k == 1:
+            before = prev[pl.ds(here, size), :]
+        else:
+            before = win[k - 2, pl.ds(there, size), :]
+        win[k, pl.ds(there, size), :] = (
+            2.0 * total - before.astype(jnp.float32)
+        ).astype(win.dtype)
+        for way in range(2):
+            halo_copy(k, way, here, size).start()
+
+    def help_piece(c, q):
         base = pl.multiple_of(q * rows, rows)
         total = jnp.dot(
-            dense[i, pl.ds(base, rows), :],
-            win[0, pl.ds(i * bs, depth), :],
+            dense[c, pl.ds(base, rows), :],
+            hwin[pl.ds(c * bs, depth), :],
             preferred_element_type=jnp.float32,
         )
-        here = pl.multiple_of(i * bs + q * rows, rows)
-        before = prev[pl.ds(here, rows), :].astype(jnp.float32)
-        win[1, pl.ds(pl.multiple_of(span + here, rows), rows), :] = (
-            2.0 * total - before
-        ).astype(win.dtype)
-        for way in range(2):
-            halo_copy(1, way, here, rows).start()
+        before = hprev[pl.ds(pl.multiple_of(c * bs + base, rows), rows), :]
+        hout[c] = (2.0 * total - before.astype(jnp.float32)).astype(hout.dtype)
+        help_copy(c).start()
+
+    def unpack(c, q, side):
+        lo, hi = chunks[c]
+        for s in range(lo, hi):
+            stage[s + side * (slots + 1)] = full[q, s]
+        base = pl.multiple_of(q * rows, rows)
+        for o in range(offs):
+            dense[c, pl.ds(base, rows), o * bs:(o + 1) * bs] = stage[
+                slot_of[c * offs + o] + side * (slots + 1)
+            ]
 
     base_z = pl.multiple_of(z * rows, rows)
     for i in range(rb):
@@ -142,11 +219,16 @@
     for way in range(2):
         halo_copy(0, way, 0, span).wait_recv()
     for i in range(rb):
-        first_step(i, z)
+        piece(1, i, base_z, rows)
 
     def hop(d, carry):
+        @pl.when(jnp.logical_and(helps, d == n_probe - 2))
+        def _():
+            lent_vec().wait_recv()
+            for way in range(2):
+                lent_halo(way).start()
+
         for c in range(rb):
-            lo, hi = chunks[c]
             for side in range(2):
                 q = z - d if side == 0 else z + d
                 valid = q >= 0 if side == 0 else q < n_probe
@@ -165,18 +247,45 @@
 
                 @pl.when(valid)
                 def _():
-                    for s in range(lo, hi):
-                        stage[s + side * (slots + 1)] = full[q, s]
-                    base = pl.multiple_of(q * rows, rows)
-                    for o in range(offs):
-                        dense[c, pl.ds(base, rows), o * bs:(o + 1) * bs] = stage[
-                            slot_of[c * offs + o] + side * (slots + 1)
-                        ]
-                    first_step(c, q)
+                    unpack(c, q, side)
+                    piece(1, c, pl.multiple_of(q * rows, rows), rows)
+
+            @pl.when(jnp.logical_and(helps, d == n_probe - 2))
+            def _():
+                if c == 0:
+                    lent_prev(0, rb * rows).wait_recv()
+                    for way in range(2):
+                        lent_halo(way).wait_recv()
+                help_piece(c, far)
         return carry
 
     stage[2 * slots + 1] = jnp.zeros((rows, bs), stage.dtype)
-    lax.fori_loop(1, n_probe, hop, 0)
+    lax.fori_loop(1, n_probe - 1, hop, 0)
+
+    @pl.when(is_end)
+    def _():
+        all_help().wait_recv()
+        base = pl.multiple_of(far * rows, rows)
+        for i in range(rb):
+            for way in range(2):
+                halo_copy(1, way, pl.multiple_of(i * bs + base, rows), rows).start()
+        for way in range(2):
+            halo_copy(1, way, 0, span).wait_recv()
+        near = pl.multiple_of(jnp.where(z == 0, 0, rows), rows)
+        for i in range(rb):
+            piece(2, i, near, bs - rows)
+        for c in range(rb):
+            lo, hi = chunks[c]
+            part = full.at[far, pl.ds(lo, hi - lo)]
+            pltpu.make_async_remote_copy(
+                src_ref=part, dst_ref=part,
+                send_sem=g_send.at[0, n_probe - 2],
+                recv_sem=g_recv.at[jnp.where(z == 0, 1, 0), n_probe - 2, c],
+                device_id=(orb, partner), device_id_type=MESH,
+            ).wait_recv()
+            unpack(c, far, 0)
+            piece(2, c, base, rows)
+
     loads[3].wait()
 
     def moment(value, start):
@@ -190,39 +299,51 @@
             preferred_element_type=jnp.float32,
         )
 
-    sums = []
-    outs = []
-    for k in range(2, STEPS + 1):
+    def own_part(k):
         for i in range(rb):
             acc[i] = dot(i, rb, rb, k - 1)
-        total = jnp.zeros((1, pc), jnp.float32)
-        for i in range(rb):
-            total += moment(win[k - 1, pl.ds(span + i * bs, bs), :], i * bs)
-        sums.append(total)
+
+    def value_of(k, i):
+        image = acc[i] + dot(i, i, rb - i, k - 1) + dot(i, 2 * rb, i + 1, k - 1)
+        before = win[k - 2, pl.ds(span + i * bs, bs), :].astype(jnp.float32)
+        return (2.0 * image - before).astype(win.dtype)
+
+    def rest_part(k):
         for way in range(2):
             halo_copy(k - 1, way, 0, span).wait_recv()
-        last_sum = jnp.zeros((1, pc), jnp.float32)
-        for i in range(rb):
-            image = acc[i] + dot(i, i, rb - i, k - 1) + dot(i, 2 * rb, i + 1, k - 1)
-            before = win[k - 2, pl.ds(span + i * bs, bs), :].astype(jnp.float32)
-            value = (2.0 * image - before).astype(win.dtype)
-            if k < STEPS:
-                win[k, pl.ds(span + i * bs, bs), :] = value
-                for way in range(2):
-                    halo_copy(k, way, i * bs, bs).start()
-            else:
-                last[pl.ds(i * bs, bs), :] = value
-                last_sum += moment(value, i * bs)
-        if k == STEPS - 1:
-            outs.append(
-                pltpu.make_async_copy(win.at[k, pl.ds(span, span)], older_hbm, out_sem.at[0])
-            )
-            outs[-1].start()
-        if k == STEPS:
-            sums.append(last_sum)
-            outs.append(pltpu.make_async_copy(last, newest_hbm, out_sem.at[1]))
-            outs[-1].start()
-
+        for i in range(rb):
+            win[k, pl.ds(span + i * bs, bs), :] = value_of(k, i)
+            for way in range(2):
+                halo_copy(k, way, i * bs, bs).start()
+
+    def step_sum(k):
+        total = jnp.zeros((1, pc), jnp.float32)
+        for i in range(rb):
+            total += moment(win[k, pl.ds(span + i * bs, bs), :], i * bs)
+        return total
+
+    @pl.when(jnp.logical_not(is_end))
+    def _():
+        own_part(2)
+        rest_part(2)
+
+    own_part(3)
+    sums = [step_sum(1), step_sum(2)]
+    rest_part(3)
+    outs = [pltpu.make_async_copy(win.at[3, pl.ds(span, span)], older_hbm, out_sem.at[0])]
+    outs[0].start()
+    own_part(4)
+    sums.append(step_sum(3))
+    for way in range(2):
+        halo_copy(3, way, 0, span).wait_recv()
+    last_sum = jnp.zeros((1, pc), jnp.float32)
+    for i in range(rb):
+        value = value_of(4, i)
+        last[pl.ds(i * bs, bs), :] = value
+        last_sum += moment(value, i * bs)
+    sums.append(last_sum)
+    outs.append(pltpu.make_async_copy(last, newest_hbm, out_sem.at[1]))
+    outs[1].start()
     mbuf[orb, 0:STEPS, :] = jnp.concatenate(sums, axis=0)
 
     def moment_copy(j):
@@ -241,6 +362,17 @@
     for k in range(STEPS):
         for way in range(2):
             halo_copy(k, way, 0, span).wait_send()
+
+    @pl.when(is_end)
+    def _():
+        lent_vec().wait_send()
+        lent_prev(0, rb * rows).wait_send()
+
+    @pl.when(helps)
+    def _():
+        for way in range(2):
+            lent_halo(way).wait_send()
+        all_help().wait_send()
 
     def sent(d, carry):
         for side in range(2):
@@ -288,7 +420,7 @@
             jax.ShapeDtypeStruct((span, pc), bf16),
             jax.ShapeDtypeStruct((STEPS, pc), f32),
         ),
-        in_specs=[pl.BlockSpec(memory_space=pltpu.SMEM)] + [anywhere] * 4,
+        in_specs=[pl.BlockSpec(memory_space=pltpu.HBM)] * 5,
         out_specs=(anywhere, anywhere, pl.BlockSpec(memory_space=pltpu.VMEM)),
         scratch_shapes=[
             pltpu.VMEM((rb * offs, rows, bs), bf16),
@@ -301,9 +433,13 @@
             pltpu.VMEM((span, pc), bf16),
             pltpu.VMEM((rb, bs, pc), f32),
             pltpu.VMEM((n_orb, 8, pc), f32),
+            pltpu.VMEM((3 * span, pc), bf16),
+            pltpu.VMEM((span, pc), bf16),
+            pltpu.VMEM((rb, rows, pc), bf16),
+            pltpu.SMEM((rb, offs), jnp.int32),
             pltpu.SMEM((rb * offs,), jnp.int32),
             pltpu.SMEM((rb * offs + 1,), jnp.int32),
-            pltpu.SemaphoreType.DMA((4,)),
+            pltpu.SemaphoreType.DMA((5,)),
             pltpu.SemaphoreType.DMA((2,)),
             pltpu.SemaphoreType.DMA((2, n_probe - 1)),
             pltpu.SemaphoreType.DMA((2, n_probe - 1, rb)),
@@ -311,9 +447,15 @@
             pltpu.SemaphoreType.DMA((STEPS, 2)),
             pltpu.SemaphoreType.DMA,
             pltpu.SemaphoreType.DMA,
+            pltpu.SemaphoreType.DMA((2,)),
+            pltpu.SemaphoreType.DMA((2,)),
+            pltpu.SemaphoreType.DMA((2,)),
+            pltpu.SemaphoreType.DMA((2,)),
+            pltpu.SemaphoreType.DMA,
+            pltpu.SemaphoreType.DMA,
         ],
         compiler_params=pltpu.CompilerParams(
-            collective_id=0, has_side_effects=True, vmem_limit_bytes=40 * 2**20
+            collective_id=0, has_side_effects=True, vmem_limit_bytes=62 * 2**20
         ),
     )(pattern, tiles.reshape(rb * offs, rows, bs), signs, previous, current)
     return older, newest, moments

time: 96.9 us -> 96.2 us (level)
  local copies, waits for them, and re-layouts: 6.87 us -> 4.59 us
  Pallas kernels: 89.1 us -> 90.7 us
    unnamed x13 -> x3, local copies, waits for them, and re-layouts: 6.87 us -> 4.59 us
    pallas_call x1, Pallas kernels: 89.1 us -> 90.7 us  [body(): pl.pallas_call(functools.partial(kernel, n_orb, n_probe, rb, offs, rows,...]
where the time goes in v2:
time: 96.2 us; the launch traced here: 95.9 us
  Pallas kernels  90.7 us (94%)
  local copies, waits for them, and re-layouts  4.59 us (5%)
    pallas_call x1, Pallas kernels, body(): pl.pallas_call(functools.partial(kernel, n_orb, n_probe, rb, offs, rows,...  90.7 us
    unnamed x3, local copies, waits for them, and re-layouts  4.59 us

profile of v2, /device:TPU:0, one launch (start us, length us, event | category | flops | bytes accessed | tf_op | source)
XLA Modules:
  0.0 95.9 jit_solution(9941735084681206734)
XLA Ops:
  0.6 90.7 %shard_map.76 = (bf16[1024,128]{1,0:T(8,128)(2,1)}, bf16[1024,128]{1,0:T(8,128)(2,1)}, f32[4,128]{1,0:T(4,128)}) custom-call(s32[4,9]{1,0:T(4,128)} %pattern_hbm.1, bf16[36,64,256]{2,1,0:T(8,128)(2,1)} %bitcast.1, s32[1024,128]{1,0:T(8,128)} %signs_hbm.1, bf16[1024,128]{1,0:T(8,128)(2,1)} %previous_hbm.1, bf16[1024,128]{1,0:T(8,128)(2,1)} %current_hbm.1), custom_call_target="tpu_custom_call" | custom-call | tf_op jit(solution)/shard_map/pallas_call | solution.py:416
  91.3 1.7 %copy.11 = bf16[1024,128]{1,0:T(8,128)(2,1)} copy(bf16[1024,128]{1,0:T(8,128)(2,1)} %get-tuple-element.6) | data formatting | bytes 524288
  93.0 1.7 %copy.12 = bf16[1024,128]{1,0:T(8,128)(2,1)} copy(bf16[1024,128]{1,0:T(8,128)(2,1)} %get-tuple-element.7) | data formatting | bytes 524288
  94.7 1.3 %copy.13 = f32[4,128]{1,0:T(4,128)} copy(f32[4,128]{1,0:T(4,128)} %get-tuple-element.8) | data formatting | bytes 4096

commit v3 on v2

--- a/solution.py
+++ b/solution.py
@@ -97,7 +97,7 @@
         to = z + 1 if side == 0 else z - 1
         return pltpu.make_async_remote_copy(
             src_ref=piece, dst_ref=piece,
-            send_sem=g_send.at[side, d - 1], recv_sem=g_recv.at[side, d - 1, c],
+            send_sem=g_send.at[side, d - 1, c], recv_sem=g_recv.at[side, d - 1, c],
             device_id=(orb, to), device_id_type=MESH,
         )
 
@@ -239,6 +239,7 @@
 
                     @pl.when(has_next[side])
                     def _():
+                        tile_copy(side, d, c, q).wait_send()
                         tile_copy(side, d + 1, c, q).start()
 
             for side in range(2):
@@ -279,7 +280,7 @@
             part = full.at[far, pl.ds(lo, hi - lo)]
             pltpu.make_async_remote_copy(
                 src_ref=part, dst_ref=part,
-                send_sem=g_send.at[0, n_probe - 2],
+                send_sem=g_send.at[0, n_probe - 2, c],
                 recv_sem=g_recv.at[jnp.where(z == 0, 1, 0), n_probe - 2, c],
                 device_id=(orb, partner), device_id_type=MESH,
             ).wait_recv()
@@ -374,21 +375,12 @@
             lent_halo(way).wait_send()
         all_help().wait_send()
 
-    def sent(d, carry):
-        for side in range(2):
-            q = z + 1 - d if side == 0 else z - 1 + d
-            valid = q >= 0 if side == 0 else q < n_probe
-
-            @pl.when(jnp.logical_and(valid, has_next[side]))
-            def _():
-                pltpu.make_async_remote_copy(
-                    src_ref=full.at[q], dst_ref=full.at[q],
-                    send_sem=g_send.at[side, d - 1], recv_sem=g_recv.at[side, d - 1, 0],
-                    device_id=(orb, z + 1 if side == 0 else z - 1), device_id_type=MESH,
-                ).wait_send()
-        return carry
-
-    lax.fori_loop(1, n_probe, sent, 0)
+    for side in range(2):
+        @pl.when(has_next[side])
+        def _():
+            final = z + 1 if side == 0 else n_probe - z
+            for c in range(rb):
+                tile_copy(side, final, c, z).wait_send()
 
     others = mbuf.at[pl.ds(0, n_orb - 1)]
     arrived = pltpu.make_async_remote_copy(
@@ -441,7 +433,7 @@
             pltpu.SMEM((rb * offs + 1,), jnp.int32),
             pltpu.SemaphoreType.DMA((5,)),
             pltpu.SemaphoreType.DMA((2,)),
-            pltpu.SemaphoreType.DMA((2, n_probe - 1)),
+            pltpu.SemaphoreType.DMA((2, n_probe - 1, rb)),
             pltpu.SemaphoreType.DMA((2, n_probe - 1, rb)),
             pltpu.SemaphoreType.DMA((STEPS, 2)),
             pltpu.SemaphoreType.DMA((STEPS, 2)),

time: 96.2 us -> 96.3 us (level)
  no operation moved by 1% of the time
where the time goes in v3:
time: 96.3 us; the launch traced here: 96.1 us
  Pallas kernels  90.9 us (94%)
  local copies, waits for them, and re-layouts  4.59 us (5%)
    pallas_call x1, Pallas kernels, body(): pl.pallas_call(functools.partial(kernel, n_orb, n_probe, rb, offs, rows,...  90.9 us
    unnamed x3, local copies, waits for them, and re-layouts  4.59 us

profile of v3, /device:TPU:0, one launch (start us, length us, event | category | flops | bytes accessed | tf_op | source)
XLA Modules:
  0.0 96.1 jit_solution(14862204241446941836)
XLA Ops:
  0.6 90.9 %shard_map.76 = (bf16[1024,128]{1,0:T(8,128)(2,1)}, bf16[1024,128]{1,0:T(8,128)(2,1)}, f32[4,128]{1,0:T(4,128)}) custom-call(s32[4,9]{1,0:T(4,128)} %pattern_hbm.1, bf16[36,64,256]{2,1,0:T(8,128)(2,1)} %bitcast.1, s32[1024,128]{1,0:T(8,128)} %signs_hbm.1, bf16[1024,128]{1,0:T(8,128)(2,1)} %previous_hbm.1, bf16[1024,128]{1,0:T(8,128)(2,1)} %current_hbm.1), custom_call_target="tpu_custom_call" | custom-call | tf_op jit(solution)/shard_map/pallas_call | solution.py:408
  91.5 1.7 %copy.11 = bf16[1024,128]{1,0:T(8,128)(2,1)} copy(bf16[1024,128]{1,0:T(8,128)(2,1)} %get-tuple-element.6) | data formatting | bytes 524288
  93.2 1.7 %copy.12 = bf16[1024,128]{1,0:T(8,128)(2,1)} copy(bf16[1024,128]{1,0:T(8,128)(2,1)} %get-tuple-element.7) | data formatting | bytes 524288
  94.8 1.3 %copy.13 = f32[4,128]{1,0:T(4,128)} copy(f32[4,128]{1,0:T(4,128)} %get-tuple-element.8) | data formatting | bytes 4096
